TPU v7x, 32 devices: a whole 2x2x4 slice. The times are simulated.
32 devices in a mesh: groups: 2 (over x), row: 16 (over z, y, core).
Axes of the slice: x: 2, y: 2, z: 4, core: 2. Of those that a mesh axis runs over, the one named last changes fastest.
Arguments:
- atom_feat: bfloat16 [4096, 2, 128], P(('groups', 'row')), parts along dimension 0, may hold values from -6 to 6
- window_shift: int32 [128], P(('groups', 'row')), parts along dimension 0, may hold values from -16 to 16, as said below
- atom_token: int32 [4096], P('groups'), parts along dimension 0, may hold values from 0 to 255, as said below
- token_in: bfloat16 [512, 2, 768], P(('groups', 'row')), parts along dimension 0, may hold values from -6 to 6
- pair: bfloat16 [512, 256, 128], P(('groups', 'row')), parts along dimension 0, may hold values from -6 to 6
- key_mask: int32 [512], P('groups'), parts along dimension 0, may hold values from 0 to 1, as said below
- w_atom_query: bfloat16 [128, 128], replicated, may hold values from -2 to 2
- w_atom_key: bfloat16 [128, 128], replicated, may hold values from -2 to 2
- w_atom_value: bfloat16 [128, 128], replicated, may hold values from -0.5 to 0.5
- w_atom_out: bfloat16 [128, 128], replicated, may hold values from -0.5 to 0.5
- w_to_token: bfloat16 [128, 768], replicated, may hold values from -0.5 to 0.5
- w_query: bfloat16 [768, 768], replicated, may hold values from -0.21875 to 0.21875
- w_key: bfloat16 [768, 768], replicated, may hold values from -0.21875 to 0.21875
- w_value: bfloat16 [768, 768], replicated, may hold values from -0.21875 to 0.21875
- w_out: bfloat16 [768, 768], replicated, may hold values from -0.21875 to 0.21875
- w_bias: bfloat16 [128, 16], replicated, may hold values from -4 to 4
Outputs:
- atom_out: bfloat16 [4096, 2, 128], P(('groups', 'row')), parts along dimension 0
- token_out: bfloat16 [512, 2, 768], P(('groups', 'row')), parts along dimension 0
There are 2 independent parts, one for each index of `groups`. A program takes and returns all parts, laid end to end along the dimension named above; an argument that names none is the same for every part. Nothing has to cross between parts.
Inputs may be any that keep to these rules, and one draw needn't show every extreme that they name: `window_shift`: one entry per query block, moving its key window. `atom_token`: never falls along the atoms; token 0 starts at atom 0 and token t's first atom is 8 t + r with r from -3 to 3, and with r from 1 to 3 where t is a positive multiple of 16. `key_mask`: token 0 is always kept.
All inputs are finite; a program needn't handle non-finite values.
Results may differ from a plain program's by a relative error of at most 0.0095.
Values may be sent and summed in bfloat16 or wider, within the bound.
A program may use at most 64 MiB of HBM per device.

v0:
```python
import jax
import jax.numpy as jnp
from jax import lax
from jax.sharding import PartitionSpec as P

ATOM_HEADS = 4
QBLOCK = 32
KWIN = 128
SHIFT = 16
TOKEN_HEADS = 16


def extended(block, sides, width):
    for axis, dim in sides:
        count = lax.axis_size(axis)
        forward = [(i, i + 1) for i in range(count - 1)]
        backward = [(target, source) for source, target in forward]
        low = lax.ppermute(
            lax.slice_in_dim(block, block.shape[dim] - width, None, axis=dim), axis, forward
        )
        high = lax.ppermute(lax.slice_in_dim(block, 0, width, axis=dim), axis, backward)
        block = jnp.concatenate([low, block, high], axis=dim)
    return block


def from_behind(block, axis, distance):
    devices = range(lax.axis_size(axis))
    route = [(i - distance, i) for i in devices if i - distance in devices]
    return lax.ppermute(block, axis, route)


def layer_norm(values):
    values = values.astype(jnp.float32)
    mean = jnp.mean(values, axis=-1, keepdims=True)
    var = jnp.mean((values - mean) ** 2, axis=-1, keepdims=True)
    return (values - mean) / jnp.sqrt(var + 1e-05)


def project(values, weight):
    return jnp.einsum("asc,cd->asd", values, weight, preferred_element_type=jnp.float32)


def on_device(
    atom_feat,
    window_shift,
    atom_token,
    token_in,
    pair,
    key_mask,
    w_atom_query,
    w_atom_key,
    w_atom_value,
    w_atom_out,
    w_to_token,
    w_query,
    w_key,
    w_value,
    w_out,
    w_bias,
):
    high = lax.Precision.HIGHEST
    atom_dev, samples, width = atom_feat.shape
    tok_dev = token_in.shape[0]
    tok_width = token_in.shape[2]
    devices = lax.axis_size("row")
    rank = lax.axis_index("row")
    atom_base = rank * atom_dev
    total_atoms = atom_dev * devices
    normed = layer_norm(atom_feat).astype(jnp.bfloat16)
    query = project(normed, w_atom_query).astype(jnp.bfloat16)
    margin = (KWIN - QBLOCK) // 2
    border = margin + SHIFT
    keyed = project(normed, w_atom_key).astype(jnp.bfloat16)
    valued = project(normed, w_atom_value).astype(jnp.bfloat16)
    stacked = extended(jnp.stack([keyed, valued], 0), (("row", 1),), border)
    key_pad = stacked[0]
    value_pad = stacked[1]
    blocks = atom_dev // QBLOCK
    starts = jnp.arange(blocks, dtype=jnp.int32) * QBLOCK - margin + window_shift
    places = starts[:, None] + jnp.arange(KWIN, dtype=jnp.int32)[None, :]
    absolute = places + atom_base
    valid = (absolute >= 0) & (absolute < total_atoms)
    window_k = jnp.take(key_pad, places + border, axis=0)
    window_v = jnp.take(value_pad, places + border, axis=0)
    head_dim = width // ATOM_HEADS
    qblock = query.reshape(blocks, QBLOCK, samples, ATOM_HEADS, head_dim)
    kblock = window_k.reshape(blocks, KWIN, samples, ATOM_HEADS, head_dim)
    vblock = window_v.reshape(blocks, KWIN, samples, ATOM_HEADS, head_dim)
    scores = jnp.einsum(
        "bqshd,bkshd->bshqk", qblock, kblock, preferred_element_type=jnp.float32
    ) / jnp.sqrt(jnp.float32(head_dim))
    keep = valid[:, None, None, None, :]
    scores = jnp.where(keep, scores, -1e30)
    top = jnp.max(scores, axis=-1, keepdims=True)
    expo = jnp.where(keep, jnp.exp(scores - top), 0.0)
    total = jnp.sum(expo, axis=-1)
    mixed = jnp.einsum(
        "bshqk,bkshd->bqshd", expo.astype(jnp.bfloat16), vblock, preferred_element_type=jnp.float32
    )
    mixed = mixed / jnp.transpose(total, (0, 3, 1, 2))[..., None]
    mixed = mixed.astype(jnp.bfloat16).reshape(atom_dev, samples, width)
    atom_out = (atom_feat.astype(jnp.float32) + project(mixed, w_atom_out)).astype(jnp.bfloat16)
    own_ids = rank * tok_dev + jnp.arange(tok_dev, dtype=jnp.int32)
    counts = jnp.sum((atom_token[None, :] == own_ids[:, None]).astype(jnp.float32), axis=1)
    local_ids = lax.dynamic_slice_in_dim(atom_token, atom_base, atom_dev)
    edge_rows = 8
    passed_atoms = from_behind(atom_out[:edge_rows], "row", -1)
    next_ids = lax.dynamic_slice_in_dim(atom_token, atom_base + atom_dev, edge_rows)
    rows = jnp.concatenate([atom_out, passed_atoms], axis=0)
    row_ids = jnp.concatenate([local_ids, next_ids], axis=0)
    hidden = jax.nn.relu(project(rows, w_to_token))
    onehot = (own_ids[:, None] == row_ids[None, :]).astype(jnp.float32)
    sums = jnp.einsum("ta,asd->tsd", onehot, hidden, precision=high)
    state = (token_in.astype(jnp.float32) + sums / counts[:, None, None]).astype(jnp.bfloat16)
    tnorm = layer_norm(state).astype(jnp.bfloat16)
    tdim = tok_width // TOKEN_HEADS
    tq = project(tnorm, w_query).astype(jnp.bfloat16).reshape(tok_dev, samples, TOKEN_HEADS, tdim)
    tk = project(tnorm, w_key).astype(jnp.bfloat16)
    tv = project(tnorm, w_value).astype(jnp.bfloat16)
    scale = 1.0 / jnp.sqrt(jnp.float32(tdim))
    running = jnp.full((samples, TOKEN_HEADS, tok_dev), -1e30, jnp.float32)
    kpiece = lax.all_gather(tk, "row", axis=0, tiled=True)
    vpiece = lax.all_gather(tv, "row", axis=0, tiled=True)
    count = kpiece.shape[0]
    kheads = kpiece.reshape(count, samples, TOKEN_HEADS, tdim)
    vheads = vpiece.reshape(count, samples, TOKEN_HEADS, tdim)
    bias = jnp.einsum("qkc,ch->hqk", pair, w_bias, preferred_element_type=jnp.float32)
    flags = (key_mask > 0)[None, None, None, :]
    score = (
        jnp.einsum("qshd,kshd->shqk", tq, kheads, preferred_element_type=jnp.float32) * scale
        + bias[None]
    )
    score = jnp.where(flags, score, -1e30)
    fresh = jnp.maximum(running, jnp.max(score, axis=-1))
    expo_t = jnp.where(flags, jnp.exp(score - fresh[..., None]), 0.0)
    denom = jnp.sum(expo_t, axis=-1)
    accum = jnp.einsum(
        "shqk,kshd->shqd", expo_t.astype(jnp.bfloat16), vheads, preferred_element_type=jnp.float32
    )
    running, denom, accum = (fresh, denom, accum)
    tmix = (accum / denom[..., None]).astype(jnp.bfloat16)
    tmix = jnp.transpose(tmix, (2, 0, 1, 3)).reshape(tok_dev, samples, tok_width)
    token_out = (state.astype(jnp.float32) + project(tmix, w_out)).astype(jnp.bfloat16)
    return (atom_out, token_out)


def solution(mesh):
    return jax.shard_map(
        on_device,
        mesh=mesh,
        in_specs=(
            P(("groups", "row"), None, None),
            P(("groups", "row")),
            P("groups"),
            P(("groups", "row"), None, None),
            P(("groups", "row"), None, None),
            P("groups"),
            P(),
            P(),
            P(),
            P(),
            P(),
            P(),
            P(),
            P(),
            P(),
            P(),
        ),
        out_specs=(P(("groups", "row"), None, None), P(("groups", "row"), None, None)),
        check_vma=False,
    )
```

profile of v0, /device:TPU:0, one launch (start us, length us, event | category | flops | bytes accessed | tf_op | source)
XLA Modules:
  0.0 78.8 jit_solution(695110558038212447)
XLA Ops:
  0.7 1.0 %convert_reduce_fusion = f32[128,2]{0,1:T(2,128)S(1)} fusion(bf16[128,2,128]{2,1,0:T(2,128)(2,1)} %param.18), kind=kLoop, calls=%fused_computation.55 | loop fusion | flops 65280 | bytes 66560 | tf_op jit(solution)/shard_map/reduce_sum | solution.py:34
  1.7 1.0 %fusion.51 = f32[128,2]{0,1:T(2,128)S(1)} fusion(f32[128,2]{0,1:T(2,128)S(1)} %broadcast_multiply_fusion.1, bf16[128,2,128]{2,1,0:T(2,128)(2,1)} %param.18), kind=kLoop, calls=%fused_computation.58 | loop fusion | flops 130816 | bytes 67584 | tf_op jit(solution)/shard_map/reduce_sum | solution.py:35
  2.8 1.2 %fusion.39 = bf16[1,128,2,128]{3,1,2,0:T(8,128)(2,1)S(1)} fusion(bf16[128,128]{1,0:T(8,128)(2,1)} %param.26, f32[128,2]{0,1:T(2,128)S(1)} %add_sqrt_fusion.1, f32[128,2]{0,1:T(2,128)S(1)} %broadcast_multiply_fusion.1, bf16[128,2,128]{2,1,0:T(2,128)(2,1)} %param.18), kind=kOutput, calls=%fused_computation.41 | convolution fusion | flops 8552448 | bytes 165888 | tf_op jit(solution)/shard_map/asc,cd->asd/dot_general | solution.py:40
  4.0 1.1 %fusion.38 = bf16[1,128,2,128]{3,1,2,0:T(8,128)(2,1)S(1)} fusion(bf16[128,128]{1,0:T(8,128)(2,1)} %param.25, f32[128,2]{0,1:T(2,128)S(1)} %add_sqrt_fusion.1, f32[128,2]{0,1:T(2,128)S(1)} %broadcast_multiply_fusion.1, bf16[128,2,128]{2,1,0:T(2,128)(2,1)} %param.18), kind=kOutput, calls=%fused_computation.40 | convolution fusion | flops 8552448 | bytes 165888 | tf_op jit(solution)/shard_map/asc,cd->asd/dot_general | solution.py:40
  5.1 2.4 %collective-permute-start = (bf16[2,64,2,128]{3,1,2,0:T(8,128)(2,1)S(1)}, bf16[2,64,2,128]{3,1,2,0:T(8,128)(2,1)S(1)}, u32[]{:S(2)}, u32[]{:S(2)}) collective-permute-start(bf16[2,64,2,128]{3,1,2,0:T(8,128)(2,1)S(1)} %get-tuple-element.11), channel_id=1, source_target_pairs={{0,1},{1,2},{2,3},{3,4},{4,5},{5,6},{6,7},{7,8},{8,9},{9,10},{10,1... | collective-permute-start | bytes 196616 | tf_op jit(solution)/shard_map/ppermute | solution.py:18
  7.5 1.3 %collective-permute-start.1 = (bf16[2,64,2,128]{3,1,2,0:T(8,128)(2,1)S(1)}, bf16[2,64,2,128]{3,1,2,0:T(8,128)(2,1)S(1)}, u32[]{:S(2)}, u32[]{:S(2)}) collective-permute-start(bf16[2,64,2,128]{3,1,2,0:T(8,128)(2,1)S(1)} %get-tuple-element.12), channel_id=1, source_target_pairs={{1,0},{2,1},{3,2},{4,3},{5,4},{6,5},{7,6},{8,7},{9,8},{10,9},{11,1... | collective-permute-start | bytes 196616 | tf_op jit(solution)/shard_map/ppermute | solution.py:21
  9.0 0.2 convolution_convert_fusion
  9.8 0.4 fusion.66
  10.2 2.6 %collective-permute-done.1 = bf16[2,64,2,128]{3,1,2,0:T(8,128)(2,1)S(1)} collective-permute-done((bf16[2,64,2,128]{3,1,2,0:T(8,128)(2,1)S(1)}, bf16[2,64,2,128]{3,1,2,0:T(8,128)(2,1)S(1)}, u32[]{:S(2)}, u32[]{:S(2)}) %collective-permute-start.1) | collective-permute-done | bytes 65568 | tf_op jit(solution)/shard_map/ppermute | solution.py:21
  13.1 2.1 %gather_fusion.1 = bf16[512,2,128]{2,1,0:T(2,128)(2,1)S(1)} fusion(bf16[256,2,128]{2,1,0:T(2,128)(2,1)S(1)} %copy.47, s32[1024]{0:T(1024)S(1)} %pad_clamp_fusion), kind=kCustom, calls=%fused_computation.1.clone | custom fusion | bytes 526336 | tf_op jit(solution)/shard_map/jit(_take)/gather | solution.py:83
  15.2 2.1 %gather_fusion = bf16[512,2,128]{2,1,0:T(2,128)(2,1)S(1)} fusion(bf16[256,2,128]{2,1,0:T(2,128)(2,1)S(1)} %copy.45, s32[1024]{0:T(1024)S(1)} %pad_clamp_fusion), kind=kCustom, calls=%fused_computation.clone | custom fusion | bytes 526336 | tf_op jit(solution)/shard_map/jit(_take)/gather | solution.py:84
  17.4 1.1 %broadcast_select_fusion = (bf16[4,128,2,128]{3,2,1,0:T(2,128)(2,1)S(1)}, bf16[4,128,2,128]{3,2,1,0:T(2,128)(2,1)S(1)}) fusion(bf16[4,128,2,128]{3,2,1,0:T(2,128)(2,1)S(1)} %bitcast.97, pred[4,128]{1,0:T(4,128)(4,1)S(1)} %get-tuple-element.16, bf16[4,128,2,128]{3,2,1,0:T(2,128)(2,1)S(1)} %bitcast.98), kind=kLoop, calls=%fused_computation.43 | loop fusion | flops 262144 | bytes 1049088 | tf_op jit(solution)/shard_map/jit(_take)/select_n | solution.py:83
  18.9 0.5 fusion.82
  19.6 0.3 fusion.8
  20.5 1.3 %collective-permute-start.2 = (bf16[8,2,128]{2,0,1:T(8,128)(2,1)S(1)}, bf16[8,2,128]{2,0,1:T(8,128)(2,1)S(1)}, u32[]{:S(2)}, u32[]{:S(2)}) collective-permute-start(bf16[8,2,128]{2,0,1:T(8,128)(2,1)S(1)} %slice.28), channel_id=1, source_target_pairs={{1,0},{2,1},{3,2},{4,3},{5,4},{6,5},{7,6},{8,7},{9,8},{10,9},{11,1... | collective-permute-start | bytes 12296 | tf_op jit(solution)/shard_map/ppermute | solution.py:29
  21.8 0.8 %copy.54 = f32[16,16,256]{2,1,0:T(8,128)} copy(f32[16,16,256]{2,0,1:T(8,128)S(1)} %fusion.66) | data formatting | bytes 524288 | tf_op jit(solution)/shard_map/qkc,ch->hqk/dot_general | solution.py:127
  22.7 0.7 copy.57
  23.4 2.6 %collective-permute-done.2 = bf16[8,2,128]{2,0,1:T(8,128)(2,1)S(1)} collective-permute-done((bf16[8,2,128]{2,0,1:T(8,128)(2,1)S(1)}, bf16[8,2,128]{2,0,1:T(8,128)(2,1)S(1)}, u32[]{:S(2)}, u32[]{:S(2)}) %collective-permute-start.2) | collective-permute-done | bytes 4128 | tf_op jit(solution)/shard_map/ppermute | solution.py:29
  26.0 0.3 convolution_maximum_fusion
  26.3 0.5 fusion.85
  27.0 0.4 fusion.29
  27.6 0.4 fusion.32
  27.9 24.9 %all_gather.6 = bf16[256,2,768]{2,0,1:T(8,128)(2,1)S(1)} all-gather(bf16[16,2,768]{2,0,1:T(8,128)(2,1)S(1)} %fusion.32), channel_id=1, replica_groups=mesh['groups'=2,'row'=16] {'row'}, dimensions={0}, use_global_device_ids=true | all-gather | bytes 835584 | tf_op jit(solution)/shard_map/all_gather | solution.py:122
  52.9 0.3 copy.52
  53.2 1.4 %fusion.86 = (f32[2,16,16]{2,1,0:T(8,128)S(1)}, f32[2,16,16,256]{3,2,1,0:T(8,128)S(1)}) fusion(f32[16,16,256]{2,1,0:T(8,128)} %copy.54, bf16[256,2,16,48]{0,3,2,1:T(8,128)(2,1)S(1)} %bitcast.96, bf16[16,2,16,48]{3,2,0,1:T(8,128)(2,1)S(1)} %reshape.96, pred[256]{0:T(512)(128)(4,1)S(1)} %broadcast_compare_fusion), kind=kOutput, calls=%fused_computation.107 | convolution fusion | flops 13106688 | bytes 1624320 | tf_op jit(solution)/shard_map/qshd,kshd->shqk/dot_general | solution.py:130
  54.5 0.4 fusion.35
  54.9 19.6 %all_gather.7 = bf16[256,2,768]{2,0,1:T(8,128)(2,1)S(1)} all-gather(bf16[16,2,768]{2,0,1:T(8,128)(2,1)S(1)} %fusion.35), channel_id=1, replica_groups=mesh['groups'=2,'row'=16] {'row'}, dimensions={0}, use_global_device_ids=true | all-gather | bytes 835584 | tf_op jit(solution)/shard_map/all_gather | solution.py:123
  74.5 1.1 %copy.55 = bf16[256,2,768]{0,2,1:T(8,128)(2,1)} copy(bf16[256,2,768]{2,0,1:T(8,128)(2,1)S(1)} %all_gather.7) | data formatting | bytes 1572864 | tf_op jit(solution)/shard_map/all_gather | solution.py:123
  75.7 0.2 fusion.40
  75.9 1.6 %fusion.18 = bf16[16,2,16,48]{3,0,2,1:T(8,128)(2,1)S(1)} fusion(bf16[256,2,16,48]{0,3,2,1:T(8,128)(2,1)} %bitcast.101, f32[2,16,16,256]{3,2,1,0:T(8,128)S(1)} %get-tuple-element.20, f32[2,16,16]{2,1,0:T(8,128)S(1)} %broadcast_maximum_fusion, pred[256]{0:T(512)(128)(4,1)S(1)} %broadcast_compare_fusion, f32[16,2,16]{0,2,1:T(8,128)S(1)} %bitcast.103), kind=kOutput, calls=%fused_computation.25 | convolution fusion | flops 13025280 | bytes 1364224 | tf_op jit(solution)/shard_map/shqk,kshd->shqd/dot_general | solution.py:137
  77.8 0.3 fusion.24
  78.1 0.7 copy.58
  (61 shorter events, 2.8 us)
Async XLA Ops:
  0.6 26.3 %copy-start = (bf16[768,768]{1,0:T(8,128)(2,1)S(1)}, bf16[768,768]{1,0:T(8,128)(2,1)}, u32[]{:S(2)}) copy-start(bf16[768,768]{1,0:T(8,128)(2,1)} %param.29) | copy-start | bytes 3538948
  0.6 8.3 %copy-start.5 = (bf16[128,2,128]{2,1,0:T(2,128)(2,1)S(1)}, bf16[128,2,128]{2,1,0:T(2,128)(2,1)}, u32[]{:S(2)}) copy-start(bf16[128,2,128]{2,1,0:T(2,128)(2,1)} %param.18) | copy-start | bytes 196612
  0.7 8.1 %copy-start.13 = (s32[4]{0:T(128)S(1)}, s32[4]{0:T(128)}, u32[]{:S(2)}) copy-start(s32[4]{0:T(128)} %param.19) | copy-start | bytes 52
  0.7 8.3 %copy-start.11 = (bf16[128,128]{1,0:T(8,128)(2,1)S(1)}, bf16[128,128]{1,0:T(8,128)(2,1)}, u32[]{:S(2)}) copy-start(bf16[128,128]{1,0:T(8,128)(2,1)} %param.24) | copy-start | bytes 98308
  2.8 6.6 %copy-start.9 = (s32[2048]{0:T(1024)S(1)}, s32[2048]{0:T(1024)}, u32[]{:S(2)}) copy-start(s32[2048]{0:T(1024)} %param.20) | copy-start | bytes 24580
  2.8 7.0 %copy-start.12 = (s32[256]{0:T(256)S(1)}, s32[256]{0:T(256)}, u32[]{:S(2)}) copy-start(s32[256]{0:T(256)} %param.23) | copy-start | bytes 3076
  2.8 7.0 %copy-start.4 = (bf16[16,256,128]{2,1,0:T(8,128)(2,1)S(1)}, bf16[16,256,128]{2,1,0:T(8,128)(2,1)}, u32[]{:S(2)}) copy-start(bf16[16,256,128]{2,1,0:T(8,128)(2,1)} %param.22) | copy-start | bytes 3145732
  2.8 7.0 %copy-start.10 = (bf16[128,16]{0,1:T(8,128)(2,1)S(1)}, bf16[128,16]{0,1:T(8,128)(2,1)}, u32[]{:S(2)}) copy-start(bf16[128,16]{0,1:T(8,128)(2,1)} %param.33) | copy-start | bytes 12292
  5.1 5.1 %collective-permute-start = (bf16[2,64,2,128]{3,1,2,0:T(8,128)(2,1)S(1)}, bf16[2,64,2,128]{3,1,2,0:T(8,128)(2,1)S(1)}, u32[]{:S(2)}, u32[]{:S(2)}) collective-permute-start(bf16[2,64,2,128]{3,1,2,0:T(8,128)(2,1)S(1)} %get-tuple-element.11), channel_id=1, source_target_pairs={{0,1},{1,2},{2,3},{3,4},{4,5},{5,6},{6,7},{7,8},{8,9},{9,10},{10,1... | collective-permute-start | bytes 196616 | tf_op jit(solution)/shard_map/ppermute | solution.py:18
  7.5 5.3 %collective-permute-start.1 = (bf16[2,64,2,128]{3,1,2,0:T(8,128)(2,1)S(1)}, bf16[2,64,2,128]{3,1,2,0:T(8,128)(2,1)S(1)}, u32[]{:S(2)}, u32[]{:S(2)}) collective-permute-start(bf16[2,64,2,128]{3,1,2,0:T(8,128)(2,1)S(1)} %get-tuple-element.12), channel_id=1, source_target_pairs={{1,0},{2,1},{3,2},{4,3},{5,4},{6,5},{7,6},{8,7},{9,8},{10,9},{11,1... | collective-permute-start | bytes 196616 | tf_op jit(solution)/shard_map/ppermute | solution.py:21
  19.6 0.8 copy-start.8
  19.9 6.1 %copy-start.6 = (bf16[128,768]{1,0:T(8,128)(2,1)S(1)}, bf16[128,768]{1,0:T(8,128)(2,1)}, u32[]{:S(2)}) copy-start(bf16[128,768]{1,0:T(8,128)(2,1)} %param.28) | copy-start | bytes 589828
  20.2 6.1 %copy-start.7 = (bf16[16,2,768]{2,1,0:T(2,128)(2,1)S(1)}, bf16[16,2,768]{2,1,0:T(2,128)(2,1)}, u32[]{:S(2)}) copy-start(bf16[16,2,768]{2,1,0:T(2,128)(2,1)} %param.21) | copy-start | bytes 147460
  20.5 5.5 %collective-permute-start.2 = (bf16[8,2,128]{2,0,1:T(8,128)(2,1)S(1)}, bf16[8,2,128]{2,0,1:T(8,128)(2,1)S(1)}, u32[]{:S(2)}, u32[]{:S(2)}) collective-permute-start(bf16[8,2,128]{2,0,1:T(8,128)(2,1)S(1)} %slice.28), channel_id=1, source_target_pairs={{1,0},{2,1},{3,2},{4,3},{5,4},{6,5},{7,6},{8,7},{9,8},{10,9},{11,1... | collective-permute-start | bytes 12296 | tf_op jit(solution)/shard_map/ppermute | solution.py:29
  26.3 1.3 %copy-start.1 = (bf16[768,768]{1,0:T(8,128)(2,1)S(1)}, bf16[768,768]{1,0:T(8,128)(2,1)}, u32[]{:S(2)}) copy-start(bf16[768,768]{1,0:T(8,128)(2,1)} %param.30) | copy-start | bytes 3538948
  53.1 1.4 %copy-start.2 = (bf16[768,768]{1,0:T(8,128)(2,1)S(1)}, bf16[768,768]{1,0:T(8,128)(2,1)}, u32[]{:S(2)}) copy-start(bf16[768,768]{1,0:T(8,128)(2,1)} %param.31) | copy-start | bytes 3538948
  75.9 1.8 %copy-start.3 = (bf16[768,768]{1,0:T(8,128)(2,1)S(1)}, bf16[768,768]{1,0:T(8,128)(2,1)}, u32[]{:S(2)}) copy-start(bf16[768,768]{1,0:T(8,128)(2,1)} %param.32) | copy-start | bytes 3538948
where the time goes:
time: 79.2 us; the launch traced here: 78.8 us
  blocking collectives  44.5 us (56%)
  local copies, waits for them, and re-layouts  9.67 us (12%)
  matrix products  9.26 us (12%)
  waiting for transfers between devices  5.23 us (7%)
  starting transfers between devices  4.94 us (6%)
  other arithmetic  4.04 us (5%)
  between operations  1.09 us (1%)
    all_gather x1, blocking collectives, on_device(): kpiece = lax.all_gather(tk, 'row', axis=0, tiled=True)  24.9 us
    all_gather x1, blocking collectives, on_device(): vpiece = lax.all_gather(tv, 'row', axis=0, tiled=True)  19.6 us
    dot_general x9, matrix products, project(): jnp.einsum('asc,cd->asd', values, weight, preferred_element_type=jnp.floa...  4.36 us
    ppermute x1, waiting for transfers between devices, from_behind(): return lax.ppermute(block, axis, route)  2.64 us
    ppermute x1, waiting for transfers between devices, extended(): lax.ppermute(lax.slice_in_dim(block, 0, width, axis=dim), axis, backward)  2.57 us
    ppermute x1, starting transfers between devices, extended(): lax.ppermute(lax.slice_in_dim(block, block.shape[dim] - width, None, axis...  2.36 us
    gather x1, local copies, waits for them, and re-layouts, on_device(): window_k = jnp.take(key_pad, places + border, axis=0)  2.11 us
    gather x1, local copies, waits for them, and re-layouts, on_device(): window_v = jnp.take(value_pad, places + border, axis=0)  2.11 us
  transfers between devices with their start and end apart: 3, of which 2 were waited for; matrix products, arithmetic and copies ran while one was open for 4% of the time, Pallas kernels for 0%

commit v1 on v0

v1 whole, which is shorter than its diff:
```python
import functools
import math

import jax
import jax.numpy as jnp
from jax import lax
from jax.experimental import pallas as pl
from jax.experimental.pallas import tpu as pltpu
from jax.sharding import PartitionSpec as P

ATOM_HEADS = 4
QBLOCK = 32
KWIN = 128
SHIFT = 16
TOKEN_HEADS = 16
LEFT = 64
RIGHT = 96
EXTRA = 16
MESH = pl.DeviceIdType.MESH
F32 = jnp.float32
BF16 = jnp.bfloat16
LOW = -1e30


def dot(a, b):
    return jnp.dot(a, b, preferred_element_type=F32)


def dot_t(a, b):
    return lax.dot_general(a, b, (((1,), (1,)), ((), ())), preferred_element_type=F32)


def normalize(values):
    mean = jnp.mean(values, axis=-1, keepdims=True)
    centred = values - mean
    var = jnp.mean(centred * centred, axis=-1, keepdims=True)
    return centred * lax.rsqrt(var + 1e-05)


def flip(index, distance):
    result = index
    bit = 1
    while bit <= distance:
        if (distance // bit) % 2:
            result = result + bit - 2 * bit * ((index // bit) % 2)
        bit *= 2
    return result


def kernel(
    n,
    shift,
    x_in,
    ids_in,
    token_in,
    pair_in,
    mask_in,
    waq_in,
    wak_in,
    wav_in,
    wao_in,
    wtt_in,
    wq_in,
    wk_in,
    wv_in,
    wo_in,
    wb_in,
    atom_out,
    token_out,
    x,
    ids,
    tin,
    pair,
    mask,
    waq,
    wak,
    wav,
    wao,
    wtt,
    wq,
    wk,
    wv,
    wo,
    wb,
    move_own,
    move_next,
    bias,
    state,
    absorbed,
    gathered,
    load_sem,
    halo_send,
    halo_recv,
    gather_send,
    gather_recv,
):
    rank = lax.axis_index("row")
    own = x_in.shape[0]
    width = waq_in.shape[0]
    samples = x_in.shape[1] // width
    tok_dev = token_in.shape[0]
    tok_width = wq_in.shape[0]
    tokens = n * tok_dev
    outers = n // 4
    core = rank % 2
    mid = (rank // 2) % 2
    outer = rank // 4

    def device(o, m, c):
        return (o * 2 + m) * 2 + c

    mid_mate = device(outer, 1 - mid, core)
    core_mate = device(outer, mid, 1 - core)

    loads = []

    def load(source, target):
        copy = pltpu.make_async_copy(source, target, load_sem.at[len(loads)])
        copy.start()
        loads.append(copy)
        return copy

    load_x = load(x_in, x.at[pl.ds(LEFT, own)])
    load_atom = [load(*p) for p in ((waq_in, waq), (wak_in, wak), (wav_in, wav))]
    load_pair = [load(wb_in, wb), load(mask_in, mask), load(pair_in, pair)]
    load_token = [load(*p) for p in ((wao_in, wao), (wtt_in, wtt), (ids_in, ids), (token_in, tin))]
    load_wq = load(wq_in, wq)
    load_wk = load(wk_in, wk)
    load_wv = load(wv_in, wv)
    load_wo = load(wo_in, wo)

    barrier = pltpu.get_barrier_semaphore()
    partners = [(rank + 1) % n, (rank + n - 1) % n, mid_mate, core_mate]
    partners += [device(flip(outer, d), mid, core) for d in range(1, outers)]
    for partner in partners:
        pl.semaphore_signal(barrier, inc=1, device_id={"row": partner}, device_id_type=MESH)
    for b in range(own // QBLOCK):
        move_own[pl.ds(8 * b, 8), :] = jnp.full((8, 128), shift[b], jnp.int32)
    pl.semaphore_wait(barrier, len(partners))

    def remote(source, target, send, recv, to):
        return pltpu.make_async_remote_copy(
            src_ref=source,
            dst_ref=target,
            send_sem=send,
            recv_sem=recv,
            device_id={"row": to},
            device_id_type=MESH,
        )

    up = (rank + 1) % n
    down = (rank + n - 1) % n
    to_right = remote(
        x_in.at[pl.ds(own - LEFT, LEFT)], x.at[pl.ds(0, LEFT)], halo_send.at[0], halo_recv.at[0], up
    )
    to_left = remote(
        x_in.at[pl.ds(0, RIGHT)],
        x.at[pl.ds(LEFT + own, RIGHT)],
        halo_send.at[1],
        halo_recv.at[1],
        down,
    )
    move_left = remote(
        move_own.at[pl.ds(0, 8)], move_next, halo_send.at[2], halo_recv.at[2], down
    )

    @pl.when(rank < n - 1)
    def _():
        to_right.start()

    @pl.when(rank > 0)
    def _():
        to_left.start()
        move_left.start()

    @pl.when(rank == 0)
    def _():
        x[pl.ds(0, LEFT), :] = jnp.zeros((LEFT, samples * width), BF16)

    @pl.when(rank == n - 1)
    def _():
        x[pl.ds(LEFT + own, RIGHT), :] = jnp.zeros((RIGHT, samples * width), BF16)
        move_next[...] = jnp.zeros((8, 128), jnp.int32)

    for copy in load_pair:
        copy.wait()
    wide = jnp.concatenate(
        [wb[...].astype(F32), jnp.zeros((wb.shape[0], 128 - TOKEN_HEADS), F32)], axis=1
    )
    wb_t = jnp.transpose(wide)[:TOKEN_HEADS].astype(BF16)
    lowered = jnp.where(mask[...] > 0, 0.0, LOW)
    for i in range(tok_dev):
        bias[:, i, :] = dot_t(wb_t, pair[i]) + lowered

    rows = own + EXTRA
    keys = LEFT + own + RIGHT
    load_x.wait()
    for copy in load_atom:
        copy.wait()

    @pl.when(rank > 0)
    def _():
        to_right.wait_recv()

    @pl.when(rank < n - 1)
    def _():
        to_left.wait_recv()
        move_left.wait_recv()

    moved = [jnp.full((QBLOCK, keys), shift[b], jnp.int32) for b in range(own // QBLOCK)]
    moved.append(jnp.broadcast_to(move_next[0:1, 0:1], (EXTRA, keys)))
    moved = jnp.concatenate(moved, axis=0)
    place = lax.broadcasted_iota(jnp.int32, (rows, keys), 1)
    query = lax.broadcasted_iota(jnp.int32, (rows, keys), 0)
    margin = (KWIN - QBLOCK) // 2
    offset = place - ((query // QBLOCK) * QBLOCK + (LEFT - margin) + moved)
    absolute = place + (rank * own - LEFT)
    keep = (offset >= 0) & (offset < KWIN) & (absolute >= 0) & (absolute < n * own)
    window = jnp.where(keep, 0.0, LOW)
    head_dim = width // ATOM_HEADS
    lane_head = lax.broadcasted_iota(jnp.int32, (rows, width), 1) // head_dim
    scale = 1.0 / math.sqrt(head_dim)
    mixes = []
    for s in range(samples):
        cols = pl.ds(s * width, width)
        normed = normalize(x[:, cols].astype(F32)).astype(BF16)
        q = dot(normed[LEFT : LEFT + rows], waq[...])
        k = dot(normed, wak[...]).astype(BF16)
        v = dot(normed, wav[...]).astype(BF16)
        stacked = jnp.concatenate(
            [jnp.where(lane_head == h, q, 0.0) for h in range(ATOM_HEADS)], axis=0
        ).astype(BF16)
        score = dot_t(stacked, k).reshape(ATOM_HEADS, rows, keys) * scale + window[None]
        expo = jnp.exp(score - jnp.max(score, axis=-1, keepdims=True))
        total = jnp.sum(expo, axis=-1, keepdims=True)
        mix = dot(expo.reshape(ATOM_HEADS * rows, keys).astype(BF16), v)
        mix = mix.reshape(ATOM_HEADS, rows, width) * (1.0 / total)
        merged = jnp.zeros((rows, width), F32)
        for h in range(ATOM_HEADS):
            merged = jnp.where(lane_head == h, mix[h], merged)
        mixes.append(merged.astype(BF16))

    for copy in load_token:
        copy.wait()
    base = rank * tok_dev
    following = jnp.where(rank < n - 1, 0, -tokens)
    own_ids = ids[pl.ds(rank, 1), :]
    next_ids = ids[pl.ds(jnp.minimum(rank + 1, n - 1), 1), :][:, :EXTRA] + following
    row_ids = jnp.concatenate([own_ids, next_ids], axis=1) - base
    member = lax.broadcasted_iota(jnp.int32, (tok_dev, rows), 0) == row_ids
    member = jnp.where(member, 1.0, 0.0)
    share = 1.0 / jnp.sum(member, axis=1, keepdims=True)
    member = member.astype(BF16)
    here = pl.ds(pl.multiple_of(rank * tok_dev, tok_dev), tok_dev)
    for s in range(samples):
        cols = pl.ds(s * width, width)
        updated = x[pl.ds(LEFT, rows), cols].astype(F32) + dot(mixes[s], wao[...])
        updated = updated.astype(BF16)
        atom_out[:, cols] = updated[:own]
        hidden = jnp.maximum(dot(updated, wtt[...]), 0.0)
        high = hidden.astype(BF16)
        low = (hidden - high.astype(F32)).astype(BF16)
        sums = dot(member, high) + dot(member, low)
        fresh = tin[:, pl.ds(s * tok_width, tok_width)].astype(F32) + sums * share
        fresh = fresh.astype(BF16)
        state[s] = fresh
        gathered[s, here, :] = normalize(fresh.astype(F32)).astype(BF16)

    sends = []

    def send_block(origin, to):
        block = gathered.at[:, pl.ds(pl.multiple_of(origin * tok_dev, tok_dev), tok_dev), :]
        copy = remote(block, block, gather_send.at[len(sends)], gather_recv.at[origin], to)
        copy.start()
        sends.append(copy)

    def await_block(origin):
        block = gathered.at[:, pl.ds(pl.multiple_of(origin * tok_dev, tok_dev), tok_dev), :]
        remote(block, block, gather_send.at[0], gather_recv.at[origin], core_mate).wait_recv()

    for d in range(1, outers):
        send_block(rank, device(flip(outer, d), mid, core))
    send_block(rank, mid_mate)
    send_block(rank, core_mate)

    tdim = tok_width // TOKEN_HEADS
    lane_token = lax.broadcasted_iota(jnp.int32, (tok_dev, tok_width), 1) // tdim
    load_wq.wait()
    load_wk.wait()
    for s in range(samples):
        q = dot(gathered[s, here, :], wq[...])
        stacked = jnp.concatenate(
            [jnp.where(lane_token == h, q, 0.0) for h in range(TOKEN_HEADS)], axis=0
        ).astype(BF16)
        absorbed[s] = dot_t(stacked, wk[...]).astype(BF16)

    for d in range(1, outers):
        origin = device(flip(outer, d), mid, core)
        await_block(origin)
        send_block(origin, mid_mate)
        send_block(origin, core_mate)
    for d in range(outers):
        origin = device(flip(outer, d), 1 - mid, core)
        await_block(origin)
        send_block(origin, core_mate)
    for d in range(outers):
        for m in (mid, 1 - mid):
            await_block(device(flip(outer, d), m, 1 - core))

    load_wv.wait()
    load_wo.wait()
    tscale = 1.0 / math.sqrt(tdim)
    for s in range(samples):
        score = dot_t(absorbed[s], gathered[s]) * tscale
        score = score + bias[...].reshape(TOKEN_HEADS * tok_dev, tokens)
        expo = jnp.exp(score - jnp.max(score, axis=-1, keepdims=True))
        total = jnp.sum(expo, axis=-1, keepdims=True)
        v = dot(gathered[s], wv[...]).astype(BF16)
        mix = dot(expo.astype(BF16), v) * (1.0 / total)
        merged = jnp.zeros((tok_dev, tok_width), F32)
        for h in range(TOKEN_HEADS):
            merged = jnp.where(lane_token == h, mix[h * tok_dev : (h + 1) * tok_dev], merged)
        result = state[s].astype(F32) + dot(merged.astype(BF16), wo[...])
        token_out[:, pl.ds(s * tok_width, tok_width)] = result.astype(BF16)

    for copy in sends:
        copy.wait_send()

    @pl.when(rank < n - 1)
    def _():
        to_right.wait_send()

    @pl.when(rank > 0)
    def _():
        to_left.wait_send()
        move_left.wait_send()


def on_device(
    n,
    atom_feat,
    window_shift,
    atom_token,
    token_in,
    pair,
    key_mask,
    w_atom_query,
    w_atom_key,
    w_atom_value,
    w_atom_out,
    w_to_token,
    w_query,
    w_key,
    w_value,
    w_out,
    w_bias,
):
    own, samples, width = atom_feat.shape
    tok_dev, _, tok_width = token_in.shape
    tokens = pair.shape[1]
    x = atom_feat.reshape(own, samples * width)
    tin = token_in.reshape(tok_dev, samples * tok_width)
    ids = atom_token.reshape(n, own)
    mask = key_mask.reshape(1, tokens)
    big = (x, ids, tin, pair, mask, w_atom_query, w_atom_key, w_atom_value, w_atom_out)
    big += (w_to_token, w_query, w_key, w_value, w_out, w_bias)
    buffers = [pltpu.VMEM(a.shape, a.dtype) for a in big]
    buffers[0] = pltpu.VMEM((LEFT + own + RIGHT, samples * width), BF16)
    atoms, toks = pl.pallas_call(
        functools.partial(kernel, n),
        out_shape=(
            jax.ShapeDtypeStruct(x.shape, BF16),
            jax.ShapeDtypeStruct(tin.shape, BF16),
        ),
        in_specs=[pl.BlockSpec(memory_space=pltpu.SMEM)]
        + [pl.BlockSpec(memory_space=pl.ANY)] * len(big),
        out_specs=(
            pl.BlockSpec(memory_space=pltpu.VMEM),
            pl.BlockSpec(memory_space=pltpu.VMEM),
        ),
        scratch_shapes=buffers
        + [
            pltpu.VMEM((8 * (own // QBLOCK), 128), jnp.int32),
            pltpu.VMEM((8, 128), jnp.int32),
            pltpu.VMEM((TOKEN_HEADS, tok_dev, tokens), F32),
            pltpu.VMEM((samples, tok_dev, tok_width), BF16),
            pltpu.VMEM((samples, TOKEN_HEADS * tok_dev, tok_width), BF16),
            pltpu.VMEM((samples, tokens, tok_width), BF16),
            pltpu.SemaphoreType.DMA((len(big),)),
            pltpu.SemaphoreType.DMA((3,)),
            pltpu.SemaphoreType.DMA((3,)),
            pltpu.SemaphoreType.DMA((n - 1,)),
            pltpu.SemaphoreType.DMA((n,)),
        ],
        compiler_params=pltpu.CompilerParams(
            collective_id=0, has_side_effects=True, vmem_limit_bytes=48 * 1024 * 1024
        ),
    )(window_shift, *big)
    return atoms.reshape(atom_feat.shape), toks.reshape(token_in.shape)


def solution(mesh):
    rows = P(("groups", "row"), None, None)
    return jax.shard_map(
        functools.partial(on_device, mesh.shape["row"]),
        mesh=mesh,
        in_specs=(rows, P(("groups", "row")), P("groups"), rows, rows, P("groups"))
        + (P(),) * 10,
        out_specs=(rows, rows),
        check_vma=False,
    )
```

time: 79.2 us -> 40.5 us (0.51)
  the two profiles are of different devices: /device:TPU:0 before, /device:TPU:1 now
where the time goes in v1:
time: 40.5 us; the launch traced here: 39.7 us
  Pallas kernels  24.3 us (60%)
  local copies, waits for them, and re-layouts  14.8 us (37%)
  between operations  0.66 us (2%)
    pallas_call x1, Pallas kernels, on_device(): pl.pallas_call(functools.partial(kernel, n), out_shape=(jax.ShapeDtypeStr...  24.3 us
    unnamed x27, local copies, waits for them, and re-layouts  13.5 us
    reshape x2, local copies, waits for them, and re-layouts, on_device(): return (atoms.reshape(atom_feat.shape), toks.reshape(token_in.shape))  1.29 us

profile of v1, /device:TPU:1, one launch (start us, length us, event | category | flops | bytes accessed | tf_op | source)
XLA Modules:
  0.0 39.7 jit_solution(4538902490118071234)
XLA Ops:
  0.6 0.8 %copy.18.wb_in = bf16[128,16]{1,0:T(8,128)(2,1)S(1)} copy(bf16[128,16]{0,1:T(8,128)(2,1)} %param.31) | data formatting | bytes 8192 | tf_op args[15]
  1.4 0.8 %copy.20 = bf16[2,8,2,768]{3,1,2,0:T(8,128)(2,1)S(1)} copy(bf16[2,8,2,768]{3,2,1,0:T(2,128)(2,1)} %bitcast.13) | data formatting | bytes 98304
  2.2 0.8 %copy.22 = bf16[16,8,2,128]{3,1,2,0:T(8,128)(2,1)S(1)} copy(bf16[16,8,2,128]{3,2,1,0:T(2,128)(2,1)} %bitcast.12) | data formatting | bytes 131072
  3.1 0.0 copy-start
  3.1 1.3 %copy-done = bf16[768,768]{1,0:T(8,128)(2,1)S(1)} copy-done((bf16[768,768]{1,0:T(8,128)(2,1)S(1)}, bf16[768,768]{1,0:T(8,128)(2,1)}, u32[]{:S(2)}) %copy-start) | copy-done | bytes 1179672
  4.4 0.0 copy-start.1
  4.4 1.3 %copy-done.1 = bf16[768,768]{1,0:T(8,128)(2,1)S(1)} copy-done((bf16[768,768]{1,0:T(8,128)(2,1)S(1)}, bf16[768,768]{1,0:T(8,128)(2,1)}, u32[]{:S(2)}) %copy-start.1) | copy-done | bytes 1179672
  5.6 0.0 copy-start.2
  5.6 1.3 %copy-done.2 = bf16[768,768]{1,0:T(8,128)(2,1)S(1)} copy-done((bf16[768,768]{1,0:T(8,128)(2,1)S(1)}, bf16[768,768]{1,0:T(8,128)(2,1)}, u32[]{:S(2)}) %copy-start.2) | copy-done | bytes 1179672
  6.9 0.0 copy-start.3
  6.9 1.2 %copy-done.3 = bf16[16,256,128]{2,1,0:T(8,128)(2,1)S(1)} copy-done((bf16[16,256,128]{2,1,0:T(8,128)(2,1)S(1)}, bf16[16,256,128]{2,1,0:T(8,128)(2,1)}, u32[]{:S(2)}) %copy-start.3) | copy-done | bytes 1048600
  8.1 0.0 copy-start.4
  8.1 0.9 %copy-done.4 = bf16[128,768]{1,0:T(8,128)(2,1)S(1)} copy-done((bf16[128,768]{1,0:T(8,128)(2,1)S(1)}, bf16[128,768]{1,0:T(8,128)(2,1)}, u32[]{:S(2)}) %copy-start.4) | copy-done | bytes 196632
  9.1 0.0 copy-start.5
  9.1 0.8 %copy-done.5 = bf16[128,128]{1,0:T(8,128)(2,1)S(1)} copy-done((bf16[128,128]{1,0:T(8,128)(2,1)S(1)}, bf16[128,128]{1,0:T(8,128)(2,1)}, u32[]{:S(2)}) %copy-start.5) | copy-done | bytes 32792
  9.8 0.0 copy-start.6
  9.8 0.8 %copy-done.6 = bf16[128,128]{1,0:T(8,128)(2,1)S(1)} copy-done((bf16[128,128]{1,0:T(8,128)(2,1)S(1)}, bf16[128,128]{1,0:T(8,128)(2,1)}, u32[]{:S(2)}) %copy-start.6) | copy-done | bytes 32792
  10.6 0.0 copy-start.7
  10.6 0.8 %copy-done.7 = bf16[128,128]{1,0:T(8,128)(2,1)S(1)} copy-done((bf16[128,128]{1,0:T(8,128)(2,1)S(1)}, bf16[128,128]{1,0:T(8,128)(2,1)}, u32[]{:S(2)}) %copy-start.7) | copy-done | bytes 32792
  11.3 0.0 copy-start.8
  11.3 0.8 %copy-done.8 = bf16[128,128]{1,0:T(8,128)(2,1)S(1)} copy-done((bf16[128,128]{1,0:T(8,128)(2,1)S(1)}, bf16[128,128]{1,0:T(8,128)(2,1)}, u32[]{:S(2)}) %copy-start.8) | copy-done | bytes 32792
  12.1 0.0 copy-start.9
  12.1 0.7 %copy-done.9 = s32[2048]{0:T(1024)S(1)} copy-done((s32[2048]{0:T(1024)S(1)}, s32[2048]{0:T(1024)}, u32[]{:S(2)}) %copy-start.9) | copy-done | bytes 8216
  12.8 0.0 copy-start.10
  12.8 0.7 %copy-done.10 = s32[256]{0:T(256)S(1)} copy-done((s32[256]{0:T(256)S(1)}, s32[256]{0:T(256)}, u32[]{:S(2)}) %copy-start.10) | copy-done | bytes 1048
  13.5 0.0 copy-start.11
  13.5 0.7 %copy-done.11 = s32[4]{0:T(128)S(1)} copy-done((s32[4]{0:T(128)S(1)}, s32[4]{0:T(128)}, u32[]{:S(2)}) %copy-start.11) | copy-done | bytes 40
  14.1 24.3 %shard_map.167 = (bf16[128,256]{1,0:T(8,128)(2,1)S(1)}, bf16[16,1536]{1,0:T(8,128)(2,1)S(1)}) custom-call(s32[4]{0:T(128)S(1)} %copy-done.11, bf16[128,256]{1,0:T(8,128)(2,1)S(1)} %bitcast.8, s32[16,128]{1,0:T(8,128)S(1)} %bitcast.10, bf16[16,1536]{1,0:T(8,128)(2,1)S(1)} %bitcast.9, bf16[16,256,128]{2,1,0:T(8,128)(2,1)S(1)} %copy-done.3, ...), custom_call_target="tpu_custom_call" | custom-call | tf_op jit(solution)/shard_map/pallas_call | solution.py:369
  38.4 0.7 %reshape.26 = bf16[128,2,128]{2,1,0:T(2,128)(2,1)} reshape(bf16[128,256]{1,0:T(8,128)(2,1)S(1)} %get-tuple-element.4) | data formatting | bytes 131072 | tf_op jit(solution)/shard_map/reshape | solution.py:399
  39.1 0.6 %reshape.27 = bf16[16,2,768]{2,1,0:T(2,128)(2,1)} reshape(bf16[16,1536]{1,0:T(8,128)(2,1)S(1)} %get-tuple-element.5) | data formatting | bytes 98304 | tf_op jit(solution)/shard_map/reshape | solution.py:399
Async XLA Ops:
  3.1 1.3 %copy-start = (bf16[768,768]{1,0:T(8,128)(2,1)S(1)}, bf16[768,768]{1,0:T(8,128)(2,1)}, u32[]{:S(2)}) copy-start(bf16[768,768]{1,0:T(8,128)(2,1)} %wq_in.1) | copy-start | bytes 3538948
  4.4 1.3 %copy-start.1 = (bf16[768,768]{1,0:T(8,128)(2,1)S(1)}, bf16[768,768]{1,0:T(8,128)(2,1)}, u32[]{:S(2)}) copy-start(bf16[768,768]{1,0:T(8,128)(2,1)} %wk_in.1) | copy-start | bytes 3538948
  5.6 1.3 %copy-start.2 = (bf16[768,768]{1,0:T(8,128)(2,1)S(1)}, bf16[768,768]{1,0:T(8,128)(2,1)}, u32[]{:S(2)}) copy-start(bf16[768,768]{1,0:T(8,128)(2,1)} %wv_in.1) | copy-start | bytes 3538948
  6.9 1.2 %copy-start.3 = (bf16[16,256,128]{2,1,0:T(8,128)(2,1)S(1)}, bf16[16,256,128]{2,1,0:T(8,128)(2,1)}, u32[]{:S(2)}) copy-start(bf16[16,256,128]{2,1,0:T(8,128)(2,1)} %pair_in.1) | copy-start | bytes 3145732
  8.1 0.9 %copy-start.4 = (bf16[128,768]{1,0:T(8,128)(2,1)S(1)}, bf16[128,768]{1,0:T(8,128)(2,1)}, u32[]{:S(2)}) copy-start(bf16[128,768]{1,0:T(8,128)(2,1)} %wtt_in.1) | copy-start | bytes 589828
  9.1 0.8 %copy-start.5 = (bf16[128,128]{1,0:T(8,128)(2,1)S(1)}, bf16[128,128]{1,0:T(8,128)(2,1)}, u32[]{:S(2)}) copy-start(bf16[128,128]{1,0:T(8,128)(2,1)} %waq_in.1) | copy-start | bytes 98308
  9.8 0.8 %copy-start.6 = (bf16[128,128]{1,0:T(8,128)(2,1)S(1)}, bf16[128,128]{1,0:T(8,128)(2,1)}, u32[]{:S(2)}) copy-start(bf16[128,128]{1,0:T(8,128)(2,1)} %wak_in.1) | copy-start | bytes 98308
  10.6 0.8 %copy-start.7 = (bf16[128,128]{1,0:T(8,128)(2,1)S(1)}, bf16[128,128]{1,0:T(8,128)(2,1)}, u32[]{:S(2)}) copy-start(bf16[128,128]{1,0:T(8,128)(2,1)} %wav_in.1) | copy-start | bytes 98308
  11.3 0.8 %copy-start.8 = (bf16[128,128]{1,0:T(8,128)(2,1)S(1)}, bf16[128,128]{1,0:T(8,128)(2,1)}, u32[]{:S(2)}) copy-start(bf16[128,128]{1,0:T(8,128)(2,1)} %wao_in.1) | copy-start | bytes 98308
  12.1 0.7 %copy-start.9 = (s32[2048]{0:T(1024)S(1)}, s32[2048]{0:T(1024)}, u32[]{:S(2)}) copy-start(s32[2048]{0:T(1024)} %param.18) | copy-start | bytes 24580
  12.8 0.7 %copy-start.10 = (s32[256]{0:T(256)S(1)}, s32[256]{0:T(256)}, u32[]{:S(2)}) copy-start(s32[256]{0:T(256)} %param.21) | copy-start | bytes 3076
  13.5 0.7 %copy-start.11 = (s32[4]{0:T(128)S(1)}, s32[4]{0:T(128)}, u32[]{:S(2)}) copy-start(s32[4]{0:T(128)} %shift.1) | copy-start | bytes 52

commit v2 on v1

--- a/solution.py
+++ b/solution.py
@@ -85,6 +85,8 @@
     move_own,
     move_next,
     bias,
+    atoms,
+    inner,
     state,
     absorbed,
     gathered,
@@ -97,7 +99,7 @@
     rank = lax.axis_index("row")
     own = x_in.shape[0]
     width = waq_in.shape[0]
-    samples = x_in.shape[1] // width
+    samples = x_in.shape[1]
     tok_dev = token_in.shape[0]
     tok_width = wq_in.shape[0]
     tokens = n * tok_dev
@@ -175,19 +177,16 @@
 
     @pl.when(rank == 0)
     def _():
-        x[pl.ds(0, LEFT), :] = jnp.zeros((LEFT, samples * width), BF16)
+        x[pl.ds(0, LEFT)] = jnp.zeros((LEFT, samples, width), BF16)
 
     @pl.when(rank == n - 1)
     def _():
-        x[pl.ds(LEFT + own, RIGHT), :] = jnp.zeros((RIGHT, samples * width), BF16)
+        x[pl.ds(LEFT + own, RIGHT)] = jnp.zeros((RIGHT, samples, width), BF16)
         move_next[...] = jnp.zeros((8, 128), jnp.int32)
 
     for copy in load_pair:
         copy.wait()
-    wide = jnp.concatenate(
-        [wb[...].astype(F32), jnp.zeros((wb.shape[0], 128 - TOKEN_HEADS), F32)], axis=1
-    )
-    wb_t = jnp.transpose(wide)[:TOKEN_HEADS].astype(BF16)
+    wb_t = wb[...]
     lowered = jnp.where(mask[...] > 0, 0.0, LOW)
     for i in range(tok_dev):
         bias[:, i, :] = dot_t(wb_t, pair[i]) + lowered
@@ -220,10 +219,10 @@
     head_dim = width // ATOM_HEADS
     lane_head = lax.broadcasted_iota(jnp.int32, (rows, width), 1) // head_dim
     scale = 1.0 / math.sqrt(head_dim)
+    atoms[...] = x[...].astype(F32).reshape(samples * keys, width)
     mixes = []
     for s in range(samples):
-        cols = pl.ds(s * width, width)
-        normed = normalize(x[:, cols].astype(F32)).astype(BF16)
+        normed = normalize(atoms[pl.ds(s, keys, stride=samples), :]).astype(BF16)
         q = dot(normed[LEFT : LEFT + rows], waq[...])
         k = dot(normed, wak[...]).astype(BF16)
         v = dot(normed, wav[...]).astype(BF16)
@@ -251,17 +250,23 @@
     member = jnp.where(member, 1.0, 0.0)
     share = 1.0 / jnp.sum(member, axis=1, keepdims=True)
     member = member.astype(BF16)
+    given = tin[...].astype(F32).reshape(samples * tok_dev, tok_width)
+    for c in range(tok_width // 128):
+        inner[c] = given[:, c * 128 : (c + 1) * 128]
     here = pl.ds(pl.multiple_of(rank * tok_dev, tok_dev), tok_dev)
     for s in range(samples):
         cols = pl.ds(s * width, width)
-        updated = x[pl.ds(LEFT, rows), cols].astype(F32) + dot(mixes[s], wao[...])
+        updated = atoms[pl.ds(LEFT * samples + s, rows, stride=samples), :] + dot(mixes[s], wao[...])
         updated = updated.astype(BF16)
         atom_out[:, cols] = updated[:own]
         hidden = jnp.maximum(dot(updated, wtt[...]), 0.0)
         high = hidden.astype(BF16)
         low = (hidden - high.astype(F32)).astype(BF16)
         sums = dot(member, high) + dot(member, low)
-        fresh = tin[:, pl.ds(s * tok_width, tok_width)].astype(F32) + sums * share
+        given = [
+            inner[c, pl.ds(s, tok_dev, stride=samples), :] for c in range(tok_width // 128)
+        ]
+        fresh = jnp.concatenate(given, axis=1) + sums * share
         fresh = fresh.astype(BF16)
         state[s] = fresh
         gathered[s, here, :] = normalize(fresh.astype(F32)).astype(BF16)
@@ -358,22 +363,20 @@
     own, samples, width = atom_feat.shape
     tok_dev, _, tok_width = token_in.shape
     tokens = pair.shape[1]
-    x = atom_feat.reshape(own, samples * width)
-    tin = token_in.reshape(tok_dev, samples * tok_width)
     ids = atom_token.reshape(n, own)
     mask = key_mask.reshape(1, tokens)
-    big = (x, ids, tin, pair, mask, w_atom_query, w_atom_key, w_atom_value, w_atom_out)
-    big += (w_to_token, w_query, w_key, w_value, w_out, w_bias)
+    big = (atom_feat, ids, token_in, pair, mask, w_atom_query, w_atom_key, w_atom_value, w_atom_out)
+    big += (w_to_token, w_query, w_key, w_value, w_out, w_bias.T)
     buffers = [pltpu.VMEM(a.shape, a.dtype) for a in big]
-    buffers[0] = pltpu.VMEM((LEFT + own + RIGHT, samples * width), BF16)
+    buffers[0] = pltpu.VMEM((LEFT + own + RIGHT, samples, width), BF16)
     atoms, toks = pl.pallas_call(
         functools.partial(kernel, n),
         out_shape=(
-            jax.ShapeDtypeStruct(x.shape, BF16),
-            jax.ShapeDtypeStruct(tin.shape, BF16),
+            jax.ShapeDtypeStruct((own, samples * width), BF16),
+            jax.ShapeDtypeStruct((tok_dev, samples * tok_width), BF16),
         ),
         in_specs=[pl.BlockSpec(memory_space=pltpu.SMEM)]
-        + [pl.BlockSpec(memory_space=pl.ANY)] * len(big),
+        + [pl.BlockSpec(memory_space=pltpu.HBM)] * len(big),
         out_specs=(
             pl.BlockSpec(memory_space=pltpu.VMEM),
             pl.BlockSpec(memory_space=pltpu.VMEM),
@@ -383,6 +386,8 @@
             pltpu.VMEM((8 * (own // QBLOCK), 128), jnp.int32),
             pltpu.VMEM((8, 128), jnp.int32),
             pltpu.VMEM((TOKEN_HEADS, tok_dev, tokens), F32),
+            pltpu.VMEM((samples * (LEFT + own + RIGHT), width), F32),
+            pltpu.VMEM((tok_width // 128, samples * tok_dev, 128), F32),
             pltpu.VMEM((samples, tok_dev, tok_width), BF16),
             pltpu.VMEM((samples, TOKEN_HEADS * tok_dev, tok_width), BF16),
             pltpu.VMEM((samples, tokens, tok_width), BF16),
@@ -393,7 +398,7 @@
             pltpu.SemaphoreType.DMA((n,)),
         ],
         compiler_params=pltpu.CompilerParams(
-            collective_id=0, has_side_effects=True, vmem_limit_bytes=48 * 1024 * 1024
+            collective_id=0, has_side_effects=True, vmem_limit_bytes=63 * 1024 * 1024
         ),
     )(window_shift, *big)
     return atoms.reshape(atom_feat.shape), toks.reshape(token_in.shape)

time: 40.5 us -> 27.7 us (0.68)
  the two profiles are of different devices: /device:TPU:1 before, /device:TPU:0 now
where the time goes in v2:
time: 27.7 us; the launch traced here: 27.3 us
  Pallas kernels  23.7 us (86%)
  local copies, waits for them, and re-layouts  2.92 us (11%)
  between operations  0.65 us (2%)
    pallas_call x1, Pallas kernels, on_device(): pl.pallas_call(functools.partial(kernel, n), out_shape=(jax.ShapeDtypeStr...  23.7 us
    reshape x2, local copies, waits for them, and re-layouts, on_device(): return (atoms.reshape(atom_feat.shape), toks.reshape(token_in.shape))  2.92 us

profile of v2, /device:TPU:0, one launch (start us, length us, event | category | flops | bytes accessed | tf_op | source)
XLA Modules:
  0.0 27.3 jit_solution(16798973100589919357)
XLA Ops:
  0.6 23.7 %shard_map.167 = (bf16[128,256]{1,0:T(8,128)(2,1)}, bf16[16,1536]{1,0:T(8,128)(2,1)}) custom-call(s32[4]{0:T(128)} %shift.1, bf16[128,2,128]{2,1,0:T(2,128)(2,1)} %x_in.1, s32[16,128]{1,0:T(8,128)} %bitcast.3, bf16[16,2,768]{2,1,0:T(2,128)(2,1)} %token_in.1, bf16[16,256,128]{2,1,0:T(8,128)(2,1)} %pair_in.1, s32[1,256]{1,0:T(1,128)} %bitcast.5, ...), custom_call_target="tpu_custom_call" | custom-call | tf_op jit(solution)/shard_map/pallas_call | solution.py:372
  24.4 1.5 %reshape.18 = bf16[128,2,128]{2,1,0:T(2,128)(2,1)} reshape(bf16[128,256]{1,0:T(8,128)(2,1)} %get-tuple-element.4) | data formatting | bytes 131072 | tf_op jit(solution)/shard_map/reshape | solution.py:404
  25.9 1.4 %reshape.19 = bf16[16,2,768]{2,1,0:T(2,128)(2,1)} reshape(bf16[16,1536]{1,0:T(8,128)(2,1)} %get-tuple-element.5) | data formatting | bytes 98304 | tf_op jit(solution)/shard_map/reshape | solution.py:404

commit v3 on v2

--- a/solution.py
+++ b/solution.py
@@ -184,13 +184,6 @@
         x[pl.ds(LEFT + own, RIGHT)] = jnp.zeros((RIGHT, samples, width), BF16)
         move_next[...] = jnp.zeros((8, 128), jnp.int32)
 
-    for copy in load_pair:
-        copy.wait()
-    wb_t = wb[...]
-    lowered = jnp.where(mask[...] > 0, 0.0, LOW)
-    for i in range(tok_dev):
-        bias[:, i, :] = dot_t(wb_t, pair[i]) + lowered
-
     rows = own + EXTRA
     keys = LEFT + own + RIGHT
     load_x.wait()
@@ -254,11 +247,29 @@
     for c in range(tok_width // 128):
         inner[c] = given[:, c * 128 : (c + 1) * 128]
     here = pl.ds(pl.multiple_of(rank * tok_dev, tok_dev), tok_dev)
+    sends = []
+
+    def block_of(s, origin):
+        return gathered.at[s, pl.ds(pl.multiple_of(origin * tok_dev, tok_dev), tok_dev), :]
+
+    def send_block(s, origin, to):
+        block = block_of(s, origin)
+        copy = remote(
+            block, block, gather_send.at[len(sends)], gather_recv.at[s * n + origin], to
+        )
+        copy.start()
+        sends.append(copy)
+
+    def await_block(s, origin):
+        block = block_of(s, origin)
+        remote(
+            block, block, gather_send.at[0], gather_recv.at[s * n + origin], core_mate
+        ).wait_recv()
+
     for s in range(samples):
-        cols = pl.ds(s * width, width)
-        updated = atoms[pl.ds(LEFT * samples + s, rows, stride=samples), :] + dot(mixes[s], wao[...])
-        updated = updated.astype(BF16)
-        atom_out[:, cols] = updated[:own]
+        updated = atoms[pl.ds(LEFT * samples + s, rows, stride=samples), :]
+        updated = (updated + dot(mixes[s], wao[...])).astype(BF16)
+        atoms[pl.ds(LEFT * samples + s, rows, stride=samples), :] = updated.astype(F32)
         hidden = jnp.maximum(dot(updated, wtt[...]), 0.0)
         high = hidden.astype(BF16)
         low = (hidden - high.astype(F32)).astype(BF16)
@@ -266,56 +277,68 @@
         given = [
             inner[c, pl.ds(s, tok_dev, stride=samples), :] for c in range(tok_width // 128)
         ]
-        fresh = jnp.concatenate(given, axis=1) + sums * share
-        fresh = fresh.astype(BF16)
+        fresh = (jnp.concatenate(given, axis=1) + sums * share).astype(BF16)
         state[s] = fresh
         gathered[s, here, :] = normalize(fresh.astype(F32)).astype(BF16)
-
-    sends = []
-
-    def send_block(origin, to):
-        block = gathered.at[:, pl.ds(pl.multiple_of(origin * tok_dev, tok_dev), tok_dev), :]
-        copy = remote(block, block, gather_send.at[len(sends)], gather_recv.at[origin], to)
-        copy.start()
-        sends.append(copy)
-
-    def await_block(origin):
-        block = gathered.at[:, pl.ds(pl.multiple_of(origin * tok_dev, tok_dev), tok_dev), :]
-        remote(block, block, gather_send.at[0], gather_recv.at[origin], core_mate).wait_recv()
-
-    for d in range(1, outers):
-        send_block(rank, device(flip(outer, d), mid, core))
-    send_block(rank, mid_mate)
-    send_block(rank, core_mate)
+        for d in range(1, outers):
+            send_block(s, rank, device(flip(outer, d), mid, core))
+        send_block(s, rank, mid_mate)
+        send_block(s, rank, core_mate)
 
     tdim = tok_width // TOKEN_HEADS
     lane_token = lax.broadcasted_iota(jnp.int32, (tok_dev, tok_width), 1) // tdim
-    load_wq.wait()
-    load_wk.wait()
-    for s in range(samples):
+
+    def absorb(s):
         q = dot(gathered[s, here, :], wq[...])
         stacked = jnp.concatenate(
             [jnp.where(lane_token == h, q, 0.0) for h in range(TOKEN_HEADS)], axis=0
         ).astype(BF16)
         absorbed[s] = dot_t(stacked, wk[...]).astype(BF16)
 
-    for d in range(1, outers):
-        origin = device(flip(outer, d), mid, core)
-        await_block(origin)
-        send_block(origin, mid_mate)
-        send_block(origin, core_mate)
-    for d in range(outers):
-        origin = device(flip(outer, d), 1 - mid, core)
-        await_block(origin)
-        send_block(origin, core_mate)
-    for d in range(outers):
-        for m in (mid, 1 - mid):
-            await_block(device(flip(outer, d), m, 1 - core))
+    def bias_rows(first, count):
+        wb_t = wb[...]
+        lowered = jnp.where(mask[...] > 0, 0.0, LOW)
+        for i in range(first, first + count):
+            bias[:, i, :] = dot_t(wb_t, pair[i]) + lowered
+
+    def relay_outer(s):
+        for d in range(1, outers):
+            origin = device(flip(outer, d), mid, core)
+            await_block(s, origin)
+            send_block(s, origin, mid_mate)
+            send_block(s, origin, core_mate)
+
+    def relay_mid(s):
+        for d in range(outers):
+            origin = device(flip(outer, d), 1 - mid, core)
+            await_block(s, origin)
+            send_block(s, origin, core_mate)
+
+    load_wq.wait()
+    load_wk.wait()
+    for copy in load_pair:
+        copy.wait()
+    quarter = tok_dev // 4
+    absorb(0)
+    relay_outer(0)
+    bias_rows(0, quarter)
+    relay_outer(1)
+    bias_rows(quarter, quarter)
+    relay_mid(0)
+    absorb(1)
+    relay_mid(1)
+    bias_rows(2 * quarter, 2 * quarter)
+    atom_out[...] = (
+        atoms[pl.ds(LEFT * samples, own * samples), :].reshape(own, samples, width).astype(BF16)
+    )
 
     load_wv.wait()
     load_wo.wait()
     tscale = 1.0 / math.sqrt(tdim)
     for s in range(samples):
+        for d in range(outers):
+            for m in (mid, 1 - mid):
+                await_block(s, device(flip(outer, d), m, 1 - core))
         score = dot_t(absorbed[s], gathered[s]) * tscale
         score = score + bias[...].reshape(TOKEN_HEADS * tok_dev, tokens)
         expo = jnp.exp(score - jnp.max(score, axis=-1, keepdims=True))
@@ -326,7 +349,10 @@
         for h in range(TOKEN_HEADS):
             merged = jnp.where(lane_token == h, mix[h * tok_dev : (h + 1) * tok_dev], merged)
         result = state[s].astype(F32) + dot(merged.astype(BF16), wo[...])
-        token_out[:, pl.ds(s * tok_width, tok_width)] = result.astype(BF16)
+        for c in range(tok_width // 128):
+            inner[c, pl.ds(s, tok_dev, stride=samples), :] = result[:, c * 128 : (c + 1) * 128]
+    result = jnp.concatenate([inner[c] for c in range(tok_width // 128)], axis=1)
+    token_out[...] = result.reshape(tok_dev, samples, tok_width).astype(BF16)
 
     for copy in sends:
         copy.wait_send()
@@ -372,8 +398,8 @@
     atoms, toks = pl.pallas_call(
         functools.partial(kernel, n),
         out_shape=(
-            jax.ShapeDtypeStruct((own, samples * width), BF16),
-            jax.ShapeDtypeStruct((tok_dev, samples * tok_width), BF16),
+            pltpu.VMEM(atom_feat.shape, BF16),
+            pltpu.VMEM(token_in.shape, BF16),
         ),
         in_specs=[pl.BlockSpec(memory_space=pltpu.SMEM)]
         + [pl.BlockSpec(memory_space=pltpu.HBM)] * len(big),
@@ -394,14 +420,14 @@
             pltpu.SemaphoreType.DMA((len(big),)),
             pltpu.SemaphoreType.DMA((3,)),
             pltpu.SemaphoreType.DMA((3,)),
-            pltpu.SemaphoreType.DMA((n - 1,)),
-            pltpu.SemaphoreType.DMA((n,)),
+            pltpu.SemaphoreType.DMA((samples * (n - 1),)),
+            pltpu.SemaphoreType.DMA((samples * n,)),
         ],
         compiler_params=pltpu.CompilerParams(
-            collective_id=0, has_side_effects=True, vmem_limit_bytes=63 * 1024 * 1024
+            collective_id=0, has_side_effects=True, vmem_limit_bytes=48 * 1024 * 1024
         ),
-    )(window_shift, *big)
-    return atoms.reshape(atom_feat.shape), toks.reshape(token_in.shape)
+    )(*[pltpu.with_memory_space_constraint(a, pltpu.HBM) for a in (window_shift, *big)])
+    return atoms, toks
 
 
 def solution(mesh):

time: 27.7 us -> 24.1 us (0.87)
  local copies, waits for them, and re-layouts: 2.92 us -> 1.25 us
  Pallas kernels: 23.7 us -> 22.1 us
    reshape x2 -> x0, local copies, waits for them, and re-layouts: 2.92 us -> none  [on_device(): return (atoms.reshape(atom_feat.shape), toks.reshape(token_in.shape))]
    pallas_call x1, Pallas kernels: 23.7 us -> 22.1 us  [on_device(): pl.pallas_call(functools.partial(kernel, n), out_shape=(pltpu.VMEM(atom_f...]
    unnamed x0 -> x2, local copies, waits for them, and re-layouts: none -> 1.25 us
where the time goes in v3:
time: 24.1 us; the launch traced here: 24 us
  Pallas kernels  22.1 us (92%)
  local copies, waits for them, and re-layouts  1.25 us (5%)
  between operations  0.65 us (3%)
    pallas_call x1, Pallas kernels, on_device(): pl.pallas_call(functools.partial(kernel, n), out_shape=(pltpu.VMEM(atom_f...  22.1 us
    unnamed x2, local copies, waits for them, and re-layouts  1.25 us

profile of v3, /device:TPU:0, one launch (start us, length us, event | category | flops | bytes accessed | tf_op | source)
XLA Modules:
  0.0 24.0 jit_solution(402507003223916686)
XLA Ops:
  0.6 22.1 %shard_map.167 = (bf16[128,2,128]{2,1,0:T(2,128)(2,1)S(1)}, bf16[16,2,768]{2,1,0:T(2,128)(2,1)S(1)}) custom-call(s32[4]{0:T(128)} %shift.1, bf16[128,2,128]{2,1,0:T(2,128)(2,1)} %x_in.1, s32[16,128]{1,0:T(8,128)} %bitcast.3, bf16[16,2,768]{2,1,0:T(2,128)(2,1)} %token_in.1, bf16[16,256,128]{2,1,0:T(8,128)(2,1)} %pair_in.1, s32[1,256]{1,0:T(1,128)} %bitcast.5, ...), custom_call_target="tpu_custom_call" | custom-call | tf_op jit(solution)/shard_map/pallas_call | solution.py:398
  22.7 0.6 %copy.20 = bf16[128,2,128]{2,1,0:T(2,128)(2,1)} copy(bf16[128,2,128]{2,1,0:T(2,128)(2,1)S(1)} %get-tuple-element.2) | data formatting | bytes 131072
  23.4 0.6 %copy.21 = bf16[16,2,768]{2,1,0:T(2,128)(2,1)} copy(bf16[16,2,768]{2,1,0:T(2,128)(2,1)S(1)} %get-tuple-element.3) | data formatting | bytes 98304

commit v4 on v3

--- a/solution.py
+++ b/solution.py
@@ -185,52 +185,55 @@
         move_next[...] = jnp.zeros((8, 128), jnp.int32)
 
     rows = own + EXTRA
-    keys = LEFT + own + RIGHT
-    load_x.wait()
-    for copy in load_atom:
-        copy.wait()
-
-    @pl.when(rank > 0)
-    def _():
-        to_right.wait_recv()
-
-    @pl.when(rank < n - 1)
-    def _():
-        to_left.wait_recv()
-        move_left.wait_recv()
-
-    moved = [jnp.full((QBLOCK, keys), shift[b], jnp.int32) for b in range(own // QBLOCK)]
-    moved.append(jnp.broadcast_to(move_next[0:1, 0:1], (EXTRA, keys)))
-    moved = jnp.concatenate(moved, axis=0)
-    place = lax.broadcasted_iota(jnp.int32, (rows, keys), 1)
-    query = lax.broadcasted_iota(jnp.int32, (rows, keys), 0)
+    reach = LEFT + own + LEFT
     margin = (KWIN - QBLOCK) // 2
-    offset = place - ((query // QBLOCK) * QBLOCK + (LEFT - margin) + moved)
-    absolute = place + (rank * own - LEFT)
-    keep = (offset >= 0) & (offset < KWIN) & (absolute >= 0) & (absolute < n * own)
-    window = jnp.where(keep, 0.0, LOW)
     head_dim = width // ATOM_HEADS
-    lane_head = lax.broadcasted_iota(jnp.int32, (rows, width), 1) // head_dim
     scale = 1.0 / math.sqrt(head_dim)
-    atoms[...] = x[...].astype(F32).reshape(samples * keys, width)
-    mixes = []
-    for s in range(samples):
-        normed = normalize(atoms[pl.ds(s, keys, stride=samples), :]).astype(BF16)
-        q = dot(normed[LEFT : LEFT + rows], waq[...])
-        k = dot(normed, wak[...]).astype(BF16)
-        v = dot(normed, wav[...]).astype(BF16)
+
+    def spread(first, count):
+        part = x[pl.ds(first, count)].astype(F32).reshape(samples * count, width)
+        atoms[pl.ds(samples * first, samples * count), :] = part
+
+    def normed_rows(s, first, count):
+        return normalize(atoms[pl.ds(samples * first + s, count, stride=samples), :]).astype(BF16)
+
+    def window(first_row, row_count, first_key, key_count, moved):
+        shape = (row_count, key_count)
+        place = lax.broadcasted_iota(jnp.int32, shape, 1) + first_key
+        query = lax.broadcasted_iota(jnp.int32, shape, 0) + first_row
+        offset = place - ((query // QBLOCK) * QBLOCK + (LEFT - margin) + moved)
+        absolute = place + (rank * own - LEFT)
+        keep = (offset >= 0) & (offset < KWIN) & (absolute >= 0) & (absolute < n * own)
+        return jnp.where(keep, 0.0, LOW)
+
+    def attend(q, k, v, lowered):
+        count, keys = lowered.shape
+        lane_head = lax.broadcasted_iota(jnp.int32, (count, width), 1) // head_dim
         stacked = jnp.concatenate(
             [jnp.where(lane_head == h, q, 0.0) for h in range(ATOM_HEADS)], axis=0
         ).astype(BF16)
-        score = dot_t(stacked, k).reshape(ATOM_HEADS, rows, keys) * scale + window[None]
+        score = dot_t(stacked, k).reshape(ATOM_HEADS, count, keys) * scale + lowered[None]
         expo = jnp.exp(score - jnp.max(score, axis=-1, keepdims=True))
         total = jnp.sum(expo, axis=-1, keepdims=True)
-        mix = dot(expo.reshape(ATOM_HEADS * rows, keys).astype(BF16), v)
-        mix = mix.reshape(ATOM_HEADS, rows, width) * (1.0 / total)
-        merged = jnp.zeros((rows, width), F32)
+        mix = dot(expo.reshape(ATOM_HEADS * count, keys).astype(BF16), v)
+        mix = mix.reshape(ATOM_HEADS, count, width) * (1.0 / total)
+        merged = jnp.zeros((count, width), F32)
         for h in range(ATOM_HEADS):
             merged = jnp.where(lane_head == h, mix[h], merged)
-        mixes.append(merged.astype(BF16))
+        return merged.astype(BF16)
+
+    load_x.wait()
+    spread(LEFT, own)
+    for copy in load_atom:
+        copy.wait()
+    q_own, k_own, v_own = [], [], []
+    for s in range(samples):
+        normed = normed_rows(s, LEFT, own)
+        q_own.append(dot(normed, waq[...]))
+        k_own.append(dot(normed, wak[...]).astype(BF16))
+        v_own.append(dot(normed, wav[...]).astype(BF16))
+    moved = [jnp.full((QBLOCK, reach), shift[b], jnp.int32) for b in range(own // QBLOCK)]
+    window_own = window(0, own, 0, reach, jnp.concatenate(moved, axis=0))
 
     for copy in load_token:
         copy.wait()
@@ -247,6 +250,40 @@
     for c in range(tok_width // 128):
         inner[c] = given[:, c * 128 : (c + 1) * 128]
     here = pl.ds(pl.multiple_of(rank * tok_dev, tok_dev), tok_dev)
+
+    @pl.when(rank > 0)
+    def _():
+        to_right.wait_recv()
+
+    @pl.when(rank < n - 1)
+    def _():
+        to_left.wait_recv()
+        move_left.wait_recv()
+
+    spread(0, LEFT)
+    spread(LEFT + own, RIGHT)
+    behind = LEFT + own - LEFT
+    ahead = LEFT + own + RIGHT - behind
+    moved = jnp.broadcast_to(move_next[0:1, 0:1], (EXTRA, ahead))
+    window_extra = window(own, EXTRA, behind, ahead, moved)
+
+    def atom_mix(s):
+        normed = jnp.concatenate(
+            [normed_rows(s, 0, LEFT), normed_rows(s, LEFT + own, RIGHT)], axis=0
+        )
+        q = dot(normed[LEFT : LEFT + EXTRA], waq[...])
+        k = dot(normed, wak[...]).astype(BF16)
+        v = dot(normed, wav[...]).astype(BF16)
+        k = jnp.concatenate([k[:LEFT], k_own[s], k[LEFT:]], axis=0)
+        v = jnp.concatenate([v[:LEFT], v_own[s], v[LEFT:]], axis=0)
+        return jnp.concatenate(
+            [
+                attend(q_own[s], k[:reach], v[:reach], window_own),
+                attend(q, k[behind:], v[behind:], window_extra),
+            ],
+            axis=0,
+        )
+
     sends = []
 
     def block_of(s, origin):
@@ -268,7 +305,7 @@
 
     for s in range(samples):
         updated = atoms[pl.ds(LEFT * samples + s, rows, stride=samples), :]
-        updated = (updated + dot(mixes[s], wao[...])).astype(BF16)
+        updated = (updated + dot(atom_mix(s), wao[...])).astype(BF16)
         atoms[pl.ds(LEFT * samples + s, rows, stride=samples), :] = updated.astype(F32)
         hidden = jnp.maximum(dot(updated, wtt[...]), 0.0)
         high = hidden.astype(BF16)
@@ -319,14 +356,14 @@
     for copy in load_pair:
         copy.wait()
     quarter = tok_dev // 4
+    relay_outer(0)
     absorb(0)
-    relay_outer(0)
+    relay_outer(1)
     bias_rows(0, quarter)
-    relay_outer(1)
+    relay_mid(0)
     bias_rows(quarter, quarter)
-    relay_mid(0)
+    relay_mid(1)
     absorb(1)
-    relay_mid(1)
     bias_rows(2 * quarter, 2 * quarter)
     atom_out[...] = (
         atoms[pl.ds(LEFT * samples, own * samples), :].reshape(own, samples, width).astype(BF16)

time: 24.1 us -> 24 us (level)
  no operation moved by 1% of the time
where the time goes in v4:
time: 24 us; the launch traced here: 23.9 us
  Pallas kernels  22 us (92%)
  local copies, waits for them, and re-layouts  1.25 us (5%)
  between operations  0.65 us (3%)
    pallas_call x1, Pallas kernels, on_device(): pl.pallas_call(functools.partial(kernel, n), out_shape=(pltpu.VMEM(atom_f...  22 us
    unnamed x2, local copies, waits for them, and re-layouts  1.25 us

profile of v4, /device:TPU:0, one launch (start us, length us, event | category | flops | bytes accessed | tf_op | source)
XLA Modules:
  0.0 23.9 jit_solution(2681300369055854811)
XLA Ops:
  0.6 22.0 %shard_map.167 = (bf16[128,2,128]{2,1,0:T(2,128)(2,1)S(1)}, bf16[16,2,768]{2,1,0:T(2,128)(2,1)S(1)}) custom-call(s32[4]{0:T(128)} %shift.1, bf16[128,2,128]{2,1,0:T(2,128)(2,1)} %x_in.1, s32[16,128]{1,0:T(8,128)} %bitcast.3, bf16[16,2,768]{2,1,0:T(2,128)(2,1)} %token_in.1, bf16[16,256,128]{2,1,0:T(8,128)(2,1)} %pair_in.1, s32[1,256]{1,0:T(1,128)} %bitcast.5, ...), custom_call_target="tpu_custom_call" | custom-call | tf_op jit(solution)/shard_map/pallas_call | solution.py:435
  22.6 0.6 %copy.20 = bf16[128,2,128]{2,1,0:T(2,128)(2,1)} copy(bf16[128,2,128]{2,1,0:T(2,128)(2,1)S(1)} %get-tuple-element.2) | data formatting | bytes 131072
  23.3 0.6 %copy.21 = bf16[16,2,768]{2,1,0:T(2,128)(2,1)} copy(bf16[16,2,768]{2,1,0:T(2,128)(2,1)S(1)} %get-tuple-element.3) | data formatting | bytes 98304

commit v5 on v4

--- a/solution.py
+++ b/solution.py
@@ -124,12 +124,7 @@
 
     load_x = load(x_in, x.at[pl.ds(LEFT, own)])
     load_atom = [load(*p) for p in ((waq_in, waq), (wak_in, wak), (wav_in, wav))]
-    load_pair = [load(wb_in, wb), load(mask_in, mask), load(pair_in, pair)]
-    load_token = [load(*p) for p in ((wao_in, wao), (wtt_in, wtt), (ids_in, ids), (token_in, tin))]
-    load_wq = load(wq_in, wq)
-    load_wk = load(wk_in, wk)
-    load_wv = load(wv_in, wv)
-    load_wo = load(wo_in, wo)
+    load_token = [load(*p) for p in ((ids_in, ids), (token_in, tin), (wao_in, wao), (wtt_in, wtt))]
 
     barrier = pltpu.get_barrier_semaphore()
     partners = [(rank + 1) % n, (rank + n - 1) % n, mid_mate, core_mate]
@@ -138,6 +133,7 @@
         pl.semaphore_signal(barrier, inc=1, device_id={"row": partner}, device_id_type=MESH)
     for b in range(own // QBLOCK):
         move_own[pl.ds(8 * b, 8), :] = jnp.full((8, 128), shift[b], jnp.int32)
+    load_x.wait()
     pl.semaphore_wait(barrier, len(partners))
 
     def remote(source, target, send, recv, to):
@@ -153,10 +149,10 @@
     up = (rank + 1) % n
     down = (rank + n - 1) % n
     to_right = remote(
-        x_in.at[pl.ds(own - LEFT, LEFT)], x.at[pl.ds(0, LEFT)], halo_send.at[0], halo_recv.at[0], up
+        x.at[pl.ds(own, LEFT)], x.at[pl.ds(0, LEFT)], halo_send.at[0], halo_recv.at[0], up
     )
     to_left = remote(
-        x_in.at[pl.ds(0, RIGHT)],
+        x.at[pl.ds(LEFT, RIGHT)],
         x.at[pl.ds(LEFT + own, RIGHT)],
         halo_send.at[1],
         halo_recv.at[1],
@@ -183,6 +179,12 @@
     def _():
         x[pl.ds(LEFT + own, RIGHT)] = jnp.zeros((RIGHT, samples, width), BF16)
         move_next[...] = jnp.zeros((8, 128), jnp.int32)
+
+    load_wq = load(wq_in, wq)
+    load_wk = load(wk_in, wk)
+    load_pair = [load(wb_in, wb), load(mask_in, mask), load(pair_in, pair)]
+    load_wv = load(wv_in, wv)
+    load_wo = load(wo_in, wo)
 
     rows = own + EXTRA
     reach = LEFT + own + LEFT
@@ -222,7 +224,6 @@
             merged = jnp.where(lane_head == h, mix[h], merged)
         return merged.astype(BF16)
 
-    load_x.wait()
     spread(LEFT, own)
     for copy in load_atom:
         copy.wait()
@@ -335,8 +336,11 @@
     def bias_rows(first, count):
         wb_t = wb[...]
         lowered = jnp.where(mask[...] > 0, 0.0, LOW)
-        for i in range(first, first + count):
-            bias[:, i, :] = dot_t(wb_t, pair[i]) + lowered
+
+        @pl.loop(first, first + count)
+        def _(i):
+            row = dot_t(wb_t, pair[i]) + lowered
+            bias[:, pl.ds(i, 1), :] = row.reshape(TOKEN_HEADS, 1, tokens)
 
     def relay_outer(s):
         for d in range(1, outers):
@@ -372,7 +376,8 @@
     load_wv.wait()
     load_wo.wait()
     tscale = 1.0 / math.sqrt(tdim)
-    for s in range(samples):
+    @pl.loop(0, samples)
+    def _(s):
         for d in range(outers):
             for m in (mid, 1 - mid):
                 await_block(s, device(flip(outer, d), m, 1 - core))
@@ -388,6 +393,7 @@
         result = state[s].astype(F32) + dot(merged.astype(BF16), wo[...])
         for c in range(tok_width // 128):
             inner[c, pl.ds(s, tok_dev, stride=samples), :] = result[:, c * 128 : (c + 1) * 128]
+
     result = jnp.concatenate([inner[c] for c in range(tok_width // 128)], axis=1)
     token_out[...] = result.reshape(tok_dev, samples, tok_width).astype(BF16)
 

time: 24 us -> 25.3 us (1.054)
  Pallas kernels: 22 us -> 23.3 us
    pallas_call x1, Pallas kernels: 22 us -> 23.3 us  [on_device(): pl.pallas_call(functools.partial(kernel, n), out_shape=(pltpu.VMEM(atom_f...]
where the time goes in v5:
time: 25.3 us; the launch traced here: 25.2 us
  Pallas kernels  23.3 us (92%)
  local copies, waits for them, and re-layouts  1.25 us (5%)
  between operations  0.65 us (3%)
    pallas_call x1, Pallas kernels, on_device(): pl.pallas_call(functools.partial(kernel, n), out_shape=(pltpu.VMEM(atom_f...  23.3 us
    unnamed x2, local copies, waits for them, and re-layouts  1.25 us

profile of v5, /device:TPU:0, one launch (start us, length us, event | category | flops | bytes accessed | tf_op | source)
XLA Modules:
  0.0 25.2 jit_solution(14744825515418777343)
XLA Ops:
  0.6 23.3 %shard_map.167 = (bf16[128,2,128]{2,1,0:T(2,128)(2,1)S(1)}, bf16[16,2,768]{2,1,0:T(2,128)(2,1)S(1)}) custom-call(s32[4]{0:T(128)} %shift.1, bf16[128,2,128]{2,1,0:T(2,128)(2,1)} %x_in.1, s32[16,128]{1,0:T(8,128)} %bitcast.3, bf16[16,2,768]{2,1,0:T(2,128)(2,1)} %token_in.1, bf16[16,256,128]{2,1,0:T(8,128)(2,1)} %pair_in.1, s32[1,256]{1,0:T(1,128)} %bitcast.5, ...), custom_call_target="tpu_custom_call" | custom-call | tf_op jit(solution)/shard_map/pallas_call | solution.py:441
  23.9 0.6 %copy.20 = bf16[128,2,128]{2,1,0:T(2,128)(2,1)} copy(bf16[128,2,128]{2,1,0:T(2,128)(2,1)S(1)} %get-tuple-element.2) | data formatting | bytes 131072
  24.5 0.6 %copy.21 = bf16[16,2,768]{2,1,0:T(2,128)(2,1)} copy(bf16[16,2,768]{2,1,0:T(2,128)(2,1)S(1)} %get-tuple-element.3) | data formatting | bytes 98304

commit v6 on v5

--- a/solution.py
+++ b/solution.py
@@ -180,9 +180,9 @@
         x[pl.ds(LEFT + own, RIGHT)] = jnp.zeros((RIGHT, samples, width), BF16)
         move_next[...] = jnp.zeros((8, 128), jnp.int32)
 
+    load_pair = [load(wb_in, wb), load(mask_in, mask), load(pair_in, pair)]
     load_wq = load(wq_in, wq)
     load_wk = load(wk_in, wk)
-    load_pair = [load(wb_in, wb), load(mask_in, mask), load(pair_in, pair)]
     load_wv = load(wv_in, wv)
     load_wo = load(wo_in, wo)
 
@@ -251,6 +251,17 @@
     for c in range(tok_width // 128):
         inner[c] = given[:, c * 128 : (c + 1) * 128]
     here = pl.ds(pl.multiple_of(rank * tok_dev, tok_dev), tok_dev)
+
+    def bias_rows(first, count):
+        wb_t = wb[...]
+        lowered = jnp.where(mask[...] > 0, 0.0, LOW)
+        for i in range(first, first + count):
+            bias[:, i, :] = dot_t(wb_t, pair[i]) + lowered
+
+    for copy in load_pair:
+        copy.wait()
+    quarter = tok_dev // 4
+    bias_rows(0, 2 * quarter)
 
     @pl.when(rank > 0)
     def _():
@@ -333,15 +344,6 @@
         ).astype(BF16)
         absorbed[s] = dot_t(stacked, wk[...]).astype(BF16)
 
-    def bias_rows(first, count):
-        wb_t = wb[...]
-        lowered = jnp.where(mask[...] > 0, 0.0, LOW)
-
-        @pl.loop(first, first + count)
-        def _(i):
-            row = dot_t(wb_t, pair[i]) + lowered
-            bias[:, pl.ds(i, 1), :] = row.reshape(TOKEN_HEADS, 1, tokens)
-
     def relay_outer(s):
         for d in range(1, outers):
             origin = device(flip(outer, d), mid, core)
@@ -355,20 +357,16 @@
             await_block(s, origin)
             send_block(s, origin, core_mate)
 
+    relay_outer(0)
     load_wq.wait()
     load_wk.wait()
-    for copy in load_pair:
-        copy.wait()
-    quarter = tok_dev // 4
-    relay_outer(0)
     absorb(0)
     relay_outer(1)
-    bias_rows(0, quarter)
+    bias_rows(2 * quarter, quarter)
     relay_mid(0)
-    bias_rows(quarter, quarter)
+    bias_rows(3 * quarter, quarter)
     relay_mid(1)
     absorb(1)
-    bias_rows(2 * quarter, 2 * quarter)
     atom_out[...] = (
         atoms[pl.ds(LEFT * samples, own * samples), :].reshape(own, samples, width).astype(BF16)
     )
@@ -376,8 +374,7 @@
     load_wv.wait()
     load_wo.wait()
     tscale = 1.0 / math.sqrt(tdim)
-    @pl.loop(0, samples)
-    def _(s):
+    for s in range(samples):
         for d in range(outers):
             for m in (mid, 1 - mid):
                 await_block(s, device(flip(outer, d), m, 1 - core))

time: 25.3 us -> 24.1 us (0.953)
  Pallas kernels: 23.3 us -> 22.1 us
    pallas_call x1, Pallas kernels: 23.3 us -> 22.1 us  [on_device(): pl.pallas_call(functools.partial(kernel, n), out_shape=(pltpu.VMEM(atom_f...]
where the time goes in v6:
time: 24.1 us; the launch traced here: 24 us
  Pallas kernels  22.1 us (92%)
  local copies, waits for them, and re-layouts  1.25 us (5%)
  between operations  0.65 us (3%)
    pallas_call x1, Pallas kernels, on_device(): pl.pallas_call(functools.partial(kernel, n), out_shape=(pltpu.VMEM(atom_f...  22.1 us
    unnamed x2, local copies, waits for them, and re-layouts  1.25 us

profile of v6, /device:TPU:0, one launch (start us, length us, event | category | flops | bytes accessed | tf_op | source)
XLA Modules:
  0.0 24.0 jit_solution(14978609460078334950)
XLA Ops:
  0.6 22.1 %shard_map.167 = (bf16[128,2,128]{2,1,0:T(2,128)(2,1)S(1)}, bf16[16,2,768]{2,1,0:T(2,128)(2,1)S(1)}) custom-call(s32[4]{0:T(128)} %shift.1, bf16[128,2,128]{2,1,0:T(2,128)(2,1)} %x_in.1, s32[16,128]{1,0:T(8,128)} %bitcast.3, bf16[16,2,768]{2,1,0:T(2,128)(2,1)} %token_in.1, bf16[16,256,128]{2,1,0:T(8,128)(2,1)} %pair_in.1, s32[1,256]{1,0:T(1,128)} %bitcast.5, ...), custom_call_target="tpu_custom_call" | custom-call | tf_op jit(solution)/shard_map/pallas_call | solution.py:438
  22.7 0.6 %copy.20 = bf16[128,2,128]{2,1,0:T(2,128)(2,1)} copy(bf16[128,2,128]{2,1,0:T(2,128)(2,1)S(1)} %get-tuple-element.2) | data formatting | bytes 131072
  23.4 0.6 %copy.21 = bf16[16,2,768]{2,1,0:T(2,128)(2,1)} copy(bf16[16,2,768]{2,1,0:T(2,128)(2,1)S(1)} %get-tuple-element.3) | data formatting | bytes 98304
